TPU v7x, 32 devices: a whole 2x2x4 slice. The times are simulated.
32 devices in a mesh: dp: 4 (over x, core), cent: 8 (over z, y).
Axes of the slice: x: 2, y: 2, z: 4, core: 2. Of those that a mesh axis runs over, the one named last changes fastest.
Arguments:
- embeddings: bfloat16 [4096, 1536], P('dp'), may hold values from -1 to 1, as said below
- sharpness: float32 [4096], P('dp'), may hold values from 10 to 300
- centroids: bfloat16 [8192, 1536], P('cent'), may hold values from -1 to 1, as said below
Outputs:
- new_centroids: float32 [8192, 1536], P('cent', 'dp')
- residuals: bfloat16 [4096, 1536], P(('dp', 'cent'))
Inputs may be any that keep to these rules, and one draw needn't show every extreme that they name: `embeddings`: each row has unit norm up to rounding. `centroids`: each row has unit norm up to rounding.
All inputs are finite; a program needn't handle non-finite values.
Results may differ from a plain program's by a relative error of at most 0.0034.
Values may be sent and summed in bfloat16 or wider, within the bound.
A program may use at most 64 MiB of HBM per device.

v0:
```python
import jax
import jax.numpy as jnp
from jax import lax
from jax.sharding import PartitionSpec as P


def per_device(embeddings, sharpness, centroids):
    scores = lax.dot_general(
        embeddings, centroids, (((1,), (1,)), ((), ())), preferred_element_type=jnp.float32
    )
    scores = scores * sharpness[:, None]
    row_top = lax.pmax(jnp.max(scores, axis=1), "cent")
    weights = jnp.exp(scores - row_top[:, None])
    row_total = lax.psum(jnp.sum(weights, axis=1), "cent")
    responsibility = (weights / row_total[:, None]).astype(jnp.bfloat16)
    partial_mixture = jnp.dot(responsibility, centroids, preferred_element_type=jnp.float32)
    share_rows = embeddings.shape[0] // lax.axis_size("cent")
    row_start = lax.axis_index("cent") * share_rows
    mixture_share = lax.psum_scatter(partial_mixture, "cent", scatter_dimension=0, tiled=True)
    own_rows = lax.dynamic_slice_in_dim(embeddings, row_start, share_rows, 0)
    own_residual = (own_rows.astype(jnp.float32) - mixture_share).astype(jnp.bfloat16)
    all_residual = lax.all_gather(own_residual, "cent", axis=0, tiled=True)
    count_part = jnp.sum(responsibility.astype(jnp.float32), axis=0)
    update = lax.dot_general(
        responsibility, all_residual, (((0,), (0,)), ((), ())), preferred_element_type=jnp.float32
    )
    width = centroids.shape[1] // lax.axis_size("dp")
    column_start = lax.axis_index("dp") * width
    centroid_cols = lax.dynamic_slice_in_dim(centroids, column_start, width, 1).astype(jnp.float32)
    counts = lax.psum(count_part, "dp")
    update_share = lax.psum_scatter(
        update.astype(jnp.bfloat16), "dp", scatter_dimension=1, tiled=True
    ).astype(jnp.float32)
    moved = centroid_cols + update_share / (counts[:, None] + 1.0)
    squares = lax.psum(jnp.sum(moved * moved, axis=1), "dp")
    new_centroids = moved * lax.rsqrt(squares + 1e-06)[:, None]
    return (new_centroids, own_residual)


def solution(mesh):
    in_specs = (P("dp", None), P("dp"), P("cent", None))
    out_specs = (P("cent", "dp"), P(("dp", "cent"), None))
    return jax.shard_map(
        per_device, mesh=mesh, in_specs=in_specs, out_specs=out_specs, check_vma=False
    )
```

profile of v0, /device:TPU:0, one launch (start us, length us, event | category | flops | bytes accessed | tf_op | source)
XLA Modules:
  0.0 311.6 jit_solution(6833034325777017204)
XLA Ops:
  7.2 0.0 reduce-scatter.5.cloned.1.call-start
  7.2 8.2 %multiply_reduce_fusion = (f32[1024]{0:T(1024)S(1)}, f32[1024,1024]{0,1:T(8,128)}) fusion(f32[1024]{0:T(1024)} %param.4, bf16[1024,1536]{1,0:T(8,128)(2,1)} %param.3, bf16[1024,1536]{1,0:T(8,128)(2,1)} %param.5), kind=kOutput, calls=%fused_computation.3 | convolution fusion | flops 3223321600 | bytes 10493952 | tf_op jit(solution)/shard_map/dot_general | solution.py:8
  15.4 23.1 %pmax.7 = f32[1024]{0:T(1024)S(1)} all-reduce(f32[1024]{0:T(1024)S(1)} %get-tuple-element.4), channel_id=1, replica_groups=mesh['dp'=4,'cent'=8] {'cent'}, use_global_device_ids=true, to_apply=%region_1.0 | all-reduce | flops 1024 | bytes 8192 | tf_op jit(solution)/shard_map/pmax | solution.py:12
  38.5 2.9 fusion
  41.5 17.1 %psum.21 = f32[1024]{0:T(1024)S(1)} all-reduce(f32[1024]{0:T(1024)S(1)} %fusion), channel_id=1, replica_groups=mesh['dp'=4,'cent'=8] {'cent'}, use_global_device_ids=true, to_apply=%region_3.0 | all-reduce | flops 1024 | bytes 8192 | tf_op jit(solution)/shard_map/psum | solution.py:14
  58.6 3.3 %convert_reduce_fusion = (f32[1024]{0:T(1024)S(1)}, bf16[1024,1024]{0,1:T(8,128)(2,1)S(1)}) fusion(f32[1024]{0:T(1024)S(1)} %psum.21, f32[1024]{0:T(1024)S(1)} %pmax.7, f32[1024,1024]{0,1:T(8,128)} %get-tuple-element.5, f32[1024]{0:T(1024)S(1)} %copy-done.2), kind=kLoop, calls=%fused_computation | loop fusion | flops 6290432 | bytes 6307840 | tf_op jit(solution)/shard_map/reduce_sum | solution.py:23
  61.9 1.3 copy-done
  63.3 5.5 %fusion.1 = f32[1024,1536]{1,0:T(8,128)} fusion(bf16[1024,1024]{0,1:T(8,128)(2,1)S(1)} %get-tuple-element.3, bf16[1024,1536]{1,0:T(8,128)(2,1)S(1)} %copy-done.1), kind=kOutput, calls=%fused_computation.12 | convolution fusion | flops 3221225472 | bytes 11534336 | tf_op jit(solution)/shard_map/dot_general | solution.py:16
  68.7 0.0 reduce-scatter.5.cloned.1.call-update
  68.8 0.0 all-gather.2.cloned.1.call-start
  68.8 116.8 %reduce-scatter.5.cloned.1.call-done = f32[128,1536]{1,0:T(8,128)} async-done(((f32[1024,1536]{1,0:T(8,128)}), f32[128,1536]{1,0:T(8,128)}) %reduce-scatter.5.cloned.1.call-update) | async-done | bytes 786448 | tf_op jit(solution)/shard_map/reduce_scatter | solution.py:19
  185.6 2.0 subtract_convert_fusion
  187.6 0.0 all-gather.2.cloned.1.call-update
  187.6 0.0 reduce-scatter.7.cloned.1.call-start
  187.7 60.3 %all-gather.2.cloned.1.call-done = bf16[1024,1536]{1,0:T(8,128)(2,1)} async-done(((bf16[128,1536]{1,0:T(8,128)(2,1)}), bf16[1024,1536]{1,0:T(8,128)(2,1)}) %all-gather.2.cloned.1.call-update) | async-done | bytes 3145744 | tf_op jit(solution)/shard_map/all_gather | solution.py:22
  248.0 5.9 %convolution_convert_fusion = bf16[1024,1536]{1,0:T(8,128)(2,1)S(1)} fusion(bf16[1024,1024]{0,1:T(8,128)(2,1)} %copy-done, bf16[1024,1536]{1,0:T(8,128)(2,1)} %all-gather.2.cloned.1.call-done), kind=kOutput, calls=%fused_computation.4 | convolution fusion | flops 3222798336 | bytes 8388608 | tf_op jit(solution)/shard_map/dot_general | solution.py:24
  253.9 2.9 copy.5
  256.8 0.0 reduce-scatter.7.cloned.1.call-update
  256.8 5.7 %psum.22 = f32[1024]{0:T(1024)S(1)} all-reduce(f32[1024]{0:T(1024)S(1)} %get-tuple-element.2), channel_id=1, replica_groups=mesh['dp'=4,'cent'=8] {'dp'}, use_global_device_ids=true, to_apply=%region_7.0 | all-reduce | flops 1024 | bytes 8192 | tf_op jit(solution)/shard_map/psum | solution.py:30
  262.6 31.0 %reduce-scatter.7.cloned.1.call-done = bf16[384,1024]{1,0:T(8,128)(2,1)} async-done(((bf16[1536,1024]{1,0:T(8,128)(2,1)}), bf16[384,1024]{1,0:T(8,128)(2,1)}) %reduce-scatter.7.cloned.1.call-update) | async-done | bytes 786448
  293.5 1.5 copy.6
  295.0 1.6 multiply_reduce_fusion.1
  296.6 5.8 %psum.23 = f32[1024]{0:T(1024)S(1)} all-reduce(f32[1024]{0:T(1024)S(1)} %multiply_reduce_fusion.1), channel_id=1, replica_groups=mesh['dp'=4,'cent'=8] {'dp'}, use_global_device_ids=true, to_apply=%region_9.0 | all-reduce | flops 1024 | bytes 8192 | tf_op jit(solution)/shard_map/psum | solution.py:35
  302.4 2.7 broadcast_multiply_fusion
  (7 shorter events, 0.0 us)
Async XLA Ops:
  7.2 31.4 %copy-start.2 = (f32[1024]{0:T(1024)S(1)}, f32[1024]{0:T(1024)}, u32[]{:S(2)}) copy-start(f32[1024]{0:T(1024)} %param.4) | copy-start | bytes 12292
  7.2 178.4 %reduce-scatter.5.cloned.1.call-start = ((), (), s32[]{:S(2)}) async-start(), calls=%async_computation.2 | async-start | bytes 7077888 | tf_op jit(solution)/shard_map/reduce_scatter | solution.py:19
  58.6 4.7 %copy-start.1 = (bf16[1024,1536]{1,0:T(8,128)(2,1)S(1)}, bf16[1024,1536]{1,0:T(8,128)(2,1)}, u32[]{:S(2)}) copy-start(bf16[1024,1536]{1,0:T(8,128)(2,1)} %param.5) | copy-start | bytes 9437188
  61.9 1.3 copy-start
  68.8 179.2 %all-gather.2.cloned.1.call-start = ((), (), s32[]{:S(2)}) async-start(), calls=%async_computation.3 | async-start | bytes 3538944 | tf_op jit(solution)/shard_map/all_gather | solution.py:22
  187.6 105.9 %reduce-scatter.7.cloned.1.call-start = ((), (), s32[]{:S(2)}) async-start(), calls=%async_computation.4 | async-start | bytes 3932160
Sparse Core Ops, SparseCore 0:
  68.9 116.6 reduce-scatter.4
  188.3 59.5 all-gather.1
  256.9 36.5 reduce-scatter.6
where the time goes:
time: 312 us
  waiting for transfers between devices  208 us (67%)
  blocking collectives  51.7 us (17%)
  matrix products  19.6 us (6%)
  between operations  13.8 us (4%)
  other arithmetic  12.6 us (4%)
  local copies, waits for them, and re-layouts  5.73 us (2%)
    reduce_scatter x1, waiting for transfers between devices, per_device(): lax.psum_scatter(partial_mixture, 'cent', scatter_dimension=0, tiled=True)  117 us
    all_gather x1, waiting for transfers between devices, per_device(): all_residual = lax.all_gather(own_residual, 'cent', axis=0, tiled=True)  60.3 us
    unnamed x4, waiting for transfers between devices  31 us
    pmax x1, blocking collectives, per_device(): row_top = lax.pmax(jnp.max(scores, axis=1), 'cent')  23.1 us
    psum x1, blocking collectives, per_device(): row_total = lax.psum(jnp.sum(weights, axis=1), 'cent')  17.1 us
    dot_general x1, matrix products, per_device(): lax.dot_general(embeddings, centroids, (((1,), (1,)), ((), ())), preferre...  8.21 us
  transfers between devices with their start and end apart: 3, of which 3 were waited for; matrix products, arithmetic and copies ran while one was open for 0% of the time, Pallas kernels for 0%

commit v1 on v0

--- a/solution.py
+++ b/solution.py
@@ -1,10 +1,17 @@
+import functools
+
 import jax
 import jax.numpy as jnp
 from jax import lax
+from jax.experimental import pallas as pl
+from jax.experimental.pallas import tpu as pltpu
 from jax.sharding import PartitionSpec as P
 
-
-def per_device(embeddings, sharpness, centroids):
+MESH = pl.DeviceIdType.MESH
+LANES = 128
+
+
+def per_device_plain(embeddings, sharpness, centroids):
     scores = lax.dot_general(
         embeddings, centroids, (((1,), (1,)), ((), ())), preferred_element_type=jnp.float32
     )
@@ -37,7 +44,293 @@
     return (new_centroids, own_residual)
 
 
+def remote(src, dst, send_sem, recv_sem, target):
+    return pltpu.make_async_remote_copy(
+        src_ref=src, dst_ref=dst, send_sem=send_sem, recv_sem=recv_sem,
+        device_id=target, device_id_type=MESH,
+    )
+
+
+def kernel(
+    n_dp, n_cent, emb, sharp, cent, out_cent, out_res,
+    weights, resp_t, resp, stats, y_out, y_in, y_own, z_out, z_in, z_own, res,
+    upd_out, upd_in, upd_own, cnt, sq,
+    st_s, st_r, y_s, y_r, z_s, z_r, gz_s, gz_r, gy_s, gy_r, u_s, u_r, c_s, c_r, q_s, q_r,
+):
+    f32, bf16 = jnp.float32, jnp.bfloat16
+    rows, depth = emb.shape
+    k = cent.shape[0]
+    width = depth // n_dp
+    nz = n_cent // 2
+    share = rows // n_cent
+    half = nz * share
+    i = lax.axis_index("dp")
+    j = lax.axis_index("cent")
+    z, y = j // 2, j % 2
+    partner = {"cent": z * 2 + (1 - y)}
+
+    barrier = pltpu.get_barrier_semaphore()
+    for d in range(1, n_cent):
+        pl.semaphore_signal(
+            barrier, inc=1, device_id={"cent": lax.rem(j + d, n_cent)}, device_id_type=MESH
+        )
+    for d in range(1, n_dp):
+        pl.semaphore_signal(
+            barrier, inc=1, device_id={"dp": lax.rem(i + d, n_dp)}, device_id_type=MESH
+        )
+
+    block = 2 * LANES if rows % (2 * LANES) == 0 else LANES
+
+    def score_block(b, _):
+        at = pl.ds(pl.multiple_of(b * block, block), block)
+        s = lax.dot_general(
+            cent[...], emb[at, :], (((1,), (1,)), ((), ())), preferred_element_type=f32
+        ) * sharp[:, at]
+        top = jnp.max(s, axis=0, keepdims=True)
+        w = jnp.exp(s - top)
+        weights[:, at] = w
+        stats[j, 0:1, at] = top
+        stats[j, 1:2, at] = jnp.sum(w, axis=0, keepdims=True)
+        return 0
+
+    lax.fori_loop(0, rows // block, score_block, 0)
+
+    pl.semaphore_wait(barrier, n_cent - 1 + n_dp - 1)
+    pending = []
+    arrivals = []
+    for d in range(1, n_cent):
+        copy = remote(
+            stats.at[j], stats.at[j], st_s.at[d - 1], st_r.at[d - 1],
+            {"cent": lax.rem(j + d, n_cent)},
+        )
+        copy.start()
+        pending.append(copy)
+    for d in range(1, n_cent):
+        src = lax.rem(j + n_cent - d, n_cent)
+        remote(stats.at[src], stats.at[src], st_s.at[d - 1], st_r.at[d - 1], partner).wait_recv()
+
+    tops = [stats[c, 0:1, :] for c in range(n_cent)]
+    top = functools.reduce(jnp.maximum, tops)
+    total = functools.reduce(
+        jnp.add, [stats[c, 1:2, :] * jnp.exp(tops[c] - top) for c in range(n_cent)]
+    )
+    stats[n_cent, 0:1, :] = jnp.exp(stats[j, 0:1, :] - top) / total
+
+    def resp_block(b, _):
+        at = pl.ds(pl.multiple_of(b * share, share), share)
+        r = weights[:, at] * stats[n_cent, 0:1, at]
+        resp_t[:, at] = r.astype(bf16)
+        to = pl.ds(pl.multiple_of((b // 2) * share, share), share)
+        resp[b % 2, to, :] = r.T.astype(bf16)
+        return 0
+
+    lax.fori_loop(0, n_cent, resp_block, 0)
+
+    def columns(s):
+        owner = lax.rem(i + 1 + s, n_dp)
+        return pl.ds(pl.multiple_of(owner * width, LANES), width)
+
+    def mix(s):
+        cols = cent[:, columns(s)]
+        y_out[s] = jnp.dot(resp[1 - y], cols, preferred_element_type=f32).astype(bf16)
+        copy = remote(y_out.at[s], y_in.at[s], y_s.at[s], y_r.at[s], partner)
+        copy.start()
+        pending.append(copy)
+        y_own[s] = jnp.dot(resp[y], cols, preferred_element_type=f32).astype(bf16)
+
+    def z_reduce(s):
+        remote(y_out.at[s], y_in.at[s], y_s.at[s], y_r.at[s], partner).wait_recv()
+        z_out[s] = (y_own[s].astype(f32) + y_in[s].astype(f32)).astype(bf16)
+        for d in range(1, nz):
+            tz = lax.rem(z + d, nz)
+            src = z_out.at[s, pl.ds(pl.multiple_of(tz * share, share), share)]
+            copy = remote(
+                src, z_in.at[s, d - 1], z_s.at[s, d - 1], z_r.at[s, d - 1], {"cent": tz * 2 + y}
+            )
+            copy.start()
+            pending.append(copy)
+
+    def rows_of(block_index):
+        return pl.ds(pl.multiple_of(block_index * share, share), share)
+
+    def residual(s):
+        acc = z_out[s, rows_of(z), :].astype(f32)
+        for d in range(1, nz):
+            remote(
+                z_in.at[s, d - 1], z_in.at[s, d - 1], z_s.at[s, d - 1], z_r.at[s, d - 1], partner
+            ).wait_recv()
+            acc += z_in[s, d - 1].astype(f32)
+        value = (emb[rows_of(j), columns(s)].astype(f32) - acc).astype(bf16)
+        out_res[:, columns(s)] = value
+        res[s, rows_of(j), :] = value
+        here = res.at[s, rows_of(j)]
+        for d in range(1, nz):
+            copy = remote(
+                here, here, gz_s.at[s, d - 1], gz_r.at[s, d - 1],
+                {"cent": lax.rem(z + d, nz) * 2 + y},
+            )
+            copy.start()
+            pending.append(copy)
+        copy = remote(here, here, gy_s.at[s, 0], gy_r.at[s, 0], partner)
+        copy.start()
+        pending.append(copy)
+
+    def forward(s):
+        for d in range(1, nz):
+            sz = lax.rem(z + nz - d, nz)
+            here = res.at[s, rows_of(sz * 2 + y)]
+            remote(here, here, gz_s.at[s, d - 1], gz_r.at[s, d - 1], partner).wait_recv()
+            copy = remote(here, here, gy_s.at[s, d], gy_r.at[s, d], partner)
+            copy.start()
+            pending.append(copy)
+
+    kb = min(k, 512)
+
+    def update(s):
+        for d in range(nz):
+            sz = lax.rem(z + nz - d, nz)
+            there = res.at[s, rows_of(sz * 2 + 1 - y)]
+            remote(there, there, gy_s.at[s, d], gy_r.at[s, d], partner).wait_recv()
+
+        def step(b, _):
+            at = pl.ds(pl.multiple_of(b * kb, kb), kb)
+            u = jnp.dot(resp_t[at, :], res[s], preferred_element_type=f32)
+            if s < n_dp - 1:
+                upd_out[s, at, :] = u.astype(bf16)
+            else:
+                upd_own[at, :] = u
+            return 0
+
+        lax.fori_loop(0, k // kb, step, 0)
+        if s < n_dp - 1:
+            copy = remote(
+                upd_out.at[s], upd_in.at[s], u_s.at[s], u_r.at[s],
+                {"dp": lax.rem(i + 1 + s, n_dp)},
+            )
+            copy.start()
+            pending.append(copy)
+
+    def share_rows_dp(buf, s_sem, r_sem):
+        for d in range(1, n_dp):
+            copy = remote(
+                buf.at[0], buf.at[d], s_sem.at[d - 1], r_sem.at[d - 1],
+                {"dp": lax.rem(i + d, n_dp)},
+            )
+            copy.start()
+            pending.append(copy)
+
+    def sum_rows_dp(buf, s_sem, r_sem):
+        acc = buf[0]
+        for d in range(1, n_dp):
+            remote(
+                buf.at[0], buf.at[d], s_sem.at[d - 1], r_sem.at[d - 1],
+                {"dp": lax.rem(i + d, n_dp)},
+            ).wait_recv()
+            acc += buf[d]
+        return jnp.broadcast_to(acc[0:1], (LANES, k)).T[:, 0:1]
+
+    mix(0)
+    for s in range(1, n_dp):
+        mix(s)
+    cnt[0] = lax.dot_general(
+        jnp.ones((8, rows), bf16), resp_t[...], (((1,), (1,)), ((), ())),
+        preferred_element_type=f32,
+    )
+    share_rows_dp(cnt, c_s, c_r)
+
+    stages = (z_reduce, residual, forward, update)
+    for t in range(n_dp + len(stages) - 1):
+        for lag, stage in reversed(list(enumerate(stages))):
+            if 0 <= t - lag < n_dp:
+                stage(t - lag)
+
+    inv = 1.0 / (sum_rows_dp(cnt, c_s, c_r) + 1.0)
+    acc = upd_own[...]
+    for s in range(n_dp - 1):
+        remote(
+            upd_out.at[s], upd_in.at[s], u_s.at[s], u_r.at[s], {"dp": lax.rem(i + 1 + s, n_dp)}
+        ).wait_recv()
+        acc += upd_in[s].astype(f32)
+    own = pl.ds(pl.multiple_of(i * width, LANES), width)
+    moved = cent[:, own].astype(f32) + acc * inv
+    upd_own[...] = moved
+    squares = jnp.sum(moved * moved, axis=1, keepdims=True)
+    sq[0] = jnp.broadcast_to(squares, (k, LANES)).T[0:8]
+    share_rows_dp(sq, q_s, q_r)
+    norm = lax.rsqrt(sum_rows_dp(sq, q_s, q_r) + 1e-06)
+    out_cent[...] = upd_own[...] * norm
+    for copy in pending:
+        copy.wait_send()
+
+
+def per_device_fused(n_dp, n_cent, embeddings, sharpness, centroids):
+    f32, bf16 = jnp.float32, jnp.bfloat16
+    rows, depth = embeddings.shape
+    k = centroids.shape[0]
+    width = depth // n_dp
+    nz = n_cent // 2
+    share = rows // n_cent
+    half = nz * share
+    vmem = pl.BlockSpec(memory_space=pltpu.VMEM)
+    dma = lambda *shape: pltpu.SemaphoreType.DMA(shape)
+    pairs = lambda *shape: [dma(*shape), dma(*shape)]
+    return pl.pallas_call(
+        functools.partial(kernel, n_dp, n_cent),
+        out_shape=(
+            jax.ShapeDtypeStruct((k, width), f32),
+            jax.ShapeDtypeStruct((share, depth), bf16),
+        ),
+        in_specs=[vmem] * 3,
+        out_specs=(vmem, vmem),
+        scratch_shapes=[
+            pltpu.VMEM((k, rows), f32),
+            pltpu.VMEM((k, rows), bf16),
+            pltpu.VMEM((2, half, k), bf16),
+            pltpu.VMEM((n_cent + 1, 2, rows), f32),
+            pltpu.VMEM((n_dp, half, width), bf16),
+            pltpu.VMEM((n_dp, half, width), bf16),
+            pltpu.VMEM((n_dp, half, width), bf16),
+            pltpu.VMEM((n_dp, half, width), bf16),
+            pltpu.VMEM((n_dp, nz - 1, share, width), bf16),
+            pltpu.VMEM((8, LANES), f32),
+            pltpu.VMEM((n_dp, rows, width), bf16),
+            pltpu.VMEM((n_dp - 1, k, width), bf16),
+            pltpu.VMEM((n_dp - 1, k, width), bf16),
+            pltpu.VMEM((k, width), f32),
+            pltpu.VMEM((n_dp, 8, k), f32),
+            pltpu.VMEM((n_dp, 8, k), f32),
+        ]
+        + pairs(n_cent - 1)
+        + pairs(n_dp)
+        + pairs(n_dp, nz - 1)
+        + pairs(n_dp, nz - 1)
+        + pairs(n_dp, nz)
+        + pairs(n_dp - 1)
+        + pairs(n_dp - 1)
+        + pairs(n_dp - 1),
+        compiler_params=pltpu.CompilerParams(
+            collective_id=0, has_side_effects=True, vmem_limit_bytes=56 * 2**20
+        ),
+    )(embeddings, sharpness.reshape(1, rows), centroids)
+
+
 def solution(mesh):
+    n_dp, n_cent = mesh.shape["dp"], mesh.shape["cent"]
+
+    def per_device(embeddings, sharpness, centroids):
+        rows, depth = embeddings.shape
+        fits = (
+            n_dp > 1
+            and n_cent > 2
+            and n_cent % 2 == 0
+            and depth % (n_dp * LANES) == 0
+            and rows % (n_cent * LANES) == 0
+            and centroids.shape[0] % 512 == 0
+        )
+        if fits:
+            return per_device_fused(n_dp, n_cent, embeddings, sharpness, centroids)
+        return per_device_plain(embeddings, sharpness, centroids)
+
     in_specs = (P("dp", None), P("dp"), P("cent", None))
     out_specs = (P("cent", "dp"), P(("dp", "cent"), None))
     return jax.shard_map(

time: 312 us -> 115 us (0.37)
  waiting for transfers between devices: 208 us -> 0 us
  Pallas kernels: 0 us -> 111 us
  blocking collectives: 51.7 us -> 0 us
  matrix products: 19.6 us -> 0 us
  between operations: 13.8 us -> 0.65 us
  other arithmetic: 12.6 us -> 0 us
    reduce_scatter x1 -> x0, waiting for transfers between devices: 117 us -> none  [per_device(): lax.psum_scatter(partial_mixture, 'cent', scatter_dimension=0, tiled=True)]
    pallas_call x0 -> x1, Pallas kernels: none -> 111 us  [per_device_fused(): pl.pallas_call(functools.partial(kernel, n_dp, n_cent), out_shape=(jax.Sh...]
    all_gather x1 -> x0, waiting for transfers between devices: 60.3 us -> none  [per_device(): all_residual = lax.all_gather(own_residual, 'cent', axis=0, tiled=True)]
    unnamed x4 -> x0, waiting for transfers between devices: 31 us -> none
    psum x3 -> x0, blocking collectives: 28.6 us -> none  [the longest x1 17.1 us: per_device(): row_total = lax.psum(jnp.sum(weights, axis=1), 'cent')]
    pmax x1 -> x0, blocking collectives: 23.1 us -> none  [per_device(): row_top = lax.pmax(jnp.max(scores, axis=1), 'cent')]
    dot_general x3 -> x0, matrix products: 19.6 us -> none  [the longest x1 8.21 us: per_device(): lax.dot_general(embeddings, centroids, (((1,), (1,)), ((), ())), preferre...]
    reduce_sum x3 -> x0, other arithmetic: 7.84 us -> none  [the longest x1 3.31 us: per_device(): count_part = jnp.sum(responsibility.astype(jnp.float32), axis=0)]
  transfers between devices with their start and end apart: 3 -> 0, of which waited for: 3 -> 0; matrix products, arithmetic and copies ran while one was open for 0% -> 0% of each run, Pallas kernels for 0% -> 0%
where the time goes in v1:
time: 115 us
  Pallas kernels  111 us (97%)
  local copies, waits for them, and re-layouts  3.45 us (3%)
    pallas_call x1, Pallas kernels, per_device_fused(): pl.pallas_call(functools.partial(kernel, n_dp, n_cent), out_shape=(jax.Sh...  111 us
    unnamed x4, local copies, waits for them, and re-layouts  3.45 us

profile of v1, /device:TPU:0, one launch (start us, length us, event | category | flops | bytes accessed | tf_op | source)
XLA Modules:
  0.0 114.7 jit_solution(10339813566980769016)
XLA Ops:
  0.6 110.6 %shard_map.50 = (f32[1024,384]{1,0:T(8,128)}, bf16[128,1536]{1,0:T(8,128)(2,1)}) custom-call(bf16[1024,1536]{1,0:T(8,128)(2,1)} %emb.1, f32[1,1024]{1,0:T(1,128)} %bitcast.1, bf16[1024,1536]{1,0:T(8,128)(2,1)} %cent.1), custom_call_target="tpu_custom_call" | custom-call | tf_op jit(solution)/shard_map/pallas_call | solution.py:277
  111.3 0.0 copy-start
  111.3 2.7 %copy.7 = f32[1024,384]{1,0:T(8,128)} copy(f32[1024,384]{1,0:T(8,128)} %get-tuple-element.4) | data formatting | bytes 3145728
  114.0 0.0 copy-done
  114.0 0.7 copy.8
Async XLA Ops:
  111.3 2.7 %copy-start = (bf16[128,1536]{1,0:T(8,128)(2,1)S(1)}, bf16[128,1536]{1,0:T(8,128)(2,1)}, u32[]{:S(2)}) copy-start(bf16[128,1536]{1,0:T(8,128)(2,1)} %get-tuple-element.5) | copy-start | bytes 1179652

commit v2 on v1

v2 whole, which is shorter than its diff:
```python
import functools

import jax
import jax.numpy as jnp
from jax import lax
from jax.experimental import pallas as pl
from jax.experimental.pallas import tpu as pltpu
from jax.sharding import PartitionSpec as P

MESH = pl.DeviceIdType.MESH
LANES = 128


def per_device_plain(embeddings, sharpness, centroids):
    scores = lax.dot_general(
        embeddings, centroids, (((1,), (1,)), ((), ())), preferred_element_type=jnp.float32
    )
    scores = scores * sharpness[:, None]
    row_top = lax.pmax(jnp.max(scores, axis=1), "cent")
    weights = jnp.exp(scores - row_top[:, None])
    row_total = lax.psum(jnp.sum(weights, axis=1), "cent")
    responsibility = (weights / row_total[:, None]).astype(jnp.bfloat16)
    partial_mixture = jnp.dot(responsibility, centroids, preferred_element_type=jnp.float32)
    share_rows = embeddings.shape[0] // lax.axis_size("cent")
    row_start = lax.axis_index("cent") * share_rows
    mixture_share = lax.psum_scatter(partial_mixture, "cent", scatter_dimension=0, tiled=True)
    own_rows = lax.dynamic_slice_in_dim(embeddings, row_start, share_rows, 0)
    own_residual = (own_rows.astype(jnp.float32) - mixture_share).astype(jnp.bfloat16)
    all_residual = lax.all_gather(own_residual, "cent", axis=0, tiled=True)
    count_part = jnp.sum(responsibility.astype(jnp.float32), axis=0)
    update = lax.dot_general(
        responsibility, all_residual, (((0,), (0,)), ((), ())), preferred_element_type=jnp.float32
    )
    width = centroids.shape[1] // lax.axis_size("dp")
    column_start = lax.axis_index("dp") * width
    centroid_cols = lax.dynamic_slice_in_dim(centroids, column_start, width, 1).astype(jnp.float32)
    counts = lax.psum(count_part, "dp")
    update_share = lax.psum_scatter(
        update.astype(jnp.bfloat16), "dp", scatter_dimension=1, tiled=True
    ).astype(jnp.float32)
    moved = centroid_cols + update_share / (counts[:, None] + 1.0)
    squares = lax.psum(jnp.sum(moved * moved, axis=1), "dp")
    new_centroids = moved * lax.rsqrt(squares + 1e-06)[:, None]
    return (new_centroids, own_residual)


def remote(src, dst, send_sem, recv_sem, target):
    return pltpu.make_async_remote_copy(
        src_ref=src, dst_ref=dst, send_sem=send_sem, recv_sem=recv_sem,
        device_id=target, device_id_type=MESH,
    )


def kernel(
    n_dp, n_cent, emb, sharp, cent, out_cent, out_res,
    weights, resp_t, resp, stats, y_out, y_in, y_own, z_out, z_in, z_rel, z_acc, res,
    upd_out, upd_in, upd_own, cnt, sq,
    st_s, st_r, y_s, y_r, z_s, z_r, rl_s, rl_r, gz_s, gz_r, gf_s, gf_x, gy_s, gy_r,
    u_s, u_r, c_s, c_r, q_s, q_r,
):
    f32, bf16 = jnp.float32, jnp.bfloat16
    rows, depth = emb.shape
    k = cent.shape[0]
    width = depth // n_dp
    nz = n_cent // 2
    share = rows // n_cent
    half = nz * share
    groups = nz // 2
    pair = 2 * share
    relay = nz == 4
    i = lax.axis_index("dp")
    j = lax.axis_index("cent")
    z, y = j // 2, j % 2
    partner = {"cent": z * 2 + (1 - y)}
    inner = jnp.logical_and(z > 0, z < nz - 1)
    at_first, at_last = z == 0, z == nz - 1
    order = [nz - 1] + list(range(1, nz - 1)) if nz > 2 else [1]

    def rows_at(index):
        return pl.ds(pl.multiple_of(index * share, share), share)

    def place(zz, yy):
        return rows_at(yy * nz + zz)

    def zdev(zz):
        return {"cent": zz * 2 + y}

    barrier = pltpu.get_barrier_semaphore()
    for d in range(1, n_cent):
        pl.semaphore_signal(
            barrier, inc=1, device_id={"cent": lax.rem(j + d, n_cent)}, device_id_type=MESH
        )
    for d in range(1, n_dp):
        pl.semaphore_signal(
            barrier, inc=1, device_id={"dp": lax.rem(i + d, n_dp)}, device_id_type=MESH
        )

    pending = []

    def go(copy):
        copy.start()
        pending.append(copy.wait_send)

    def go_if(cond, copy):
        pl.when(cond)(copy.start)
        pending.append(lambda: pl.when(cond)(copy.wait_send))

    def score_group(g):
        def half_block(h, _):
            e = jnp.concatenate([emb[rows_at(4 * g + h), :], emb[rows_at(4 * g + 2 + h), :]], 0)
            sh = jnp.concatenate(
                [sharp[:, rows_at(4 * g + h)], sharp[:, rows_at(4 * g + 2 + h)]], 1
            )
            s = lax.dot_general(
                cent[...], e, (((1,), (1,)), ((), ())), preferred_element_type=f32
            ) * sh
            top = jnp.max(s, axis=0, keepdims=True)
            w = jnp.exp(s - top)
            weights[:, pl.ds(pl.multiple_of(h * half + g * pair, share), pair)] = w
            at = pl.ds(pl.multiple_of(h * pair, share), pair)
            stats[g, j, 0:1, at] = top
            stats[g, j, 1:2, at] = jnp.sum(w, axis=0, keepdims=True)
            return 0

        lax.fori_loop(0, 2, half_block, 0)

    def send_stats(g):
        here = stats.at[g, j]
        for d in range(1, n_cent):
            go(remote(
                here, here, st_s.at[g, d - 1], st_r.at[g, d - 1],
                {"cent": lax.rem(j + d, n_cent)},
            ))

    def respond(g):
        for d in range(1, n_cent):
            there = stats.at[g, lax.rem(j + n_cent - d, n_cent)]
            remote(there, there, st_s.at[g, d - 1], st_r.at[g, d - 1], partner).wait_recv()
        tops = [stats[g, c, 0:1, :] for c in range(n_cent)]
        top = functools.reduce(jnp.maximum, tops)
        total = functools.reduce(
            jnp.add, [stats[g, c, 1:2, :] * jnp.exp(tops[c] - top) for c in range(n_cent)]
        )
        stats[g, n_cent, 0:1, :] = jnp.exp(stats[g, j, 0:1, :] - top) / total

        def block(b, _):
            h, q = b // 2, b % 2
            at = place(2 * g + q, h)
            r = weights[:, at] * stats[g, n_cent, 0:1, rows_at(b)]
            resp_t[:, at] = r.astype(bf16)
            resp[h, rows_at(2 * g + q), :] = r.T.astype(bf16)
            return 0

        lax.fori_loop(0, 4, block, 0)

    def columns(s):
        owner = lax.rem(i + 1 + s, n_dp)
        return pl.ds(pl.multiple_of(owner * width, LANES), width)

    def y_copy(s, zz):
        at = rows_at(zz)
        return remote(y_out.at[s, at], y_in.at[s, at], y_s.at[s, zz], y_r.at[s, zz], partner)

    def mix_group(s, g):
        at = pl.ds(g * pair, pair)
        y_out[s, at, :] = jnp.dot(
            resp[1 - y, at, :], cent[:, columns(s)], preferred_element_type=f32
        ).astype(bf16)
        for q in range(2):
            go(y_copy(s, 2 * g + q))

    def mix_other(s):
        y_out[s] = jnp.dot(
            resp[1 - y], cent[:, columns(s)], preferred_element_type=f32
        ).astype(bf16)
        for d in order + [0]:
            go(y_copy(s, lax.rem(z + d, nz)))

    def mix_own(s):
        y_own[s] = jnp.dot(resp[y], cent[:, columns(s)], preferred_element_type=f32)

    def z_reduce(s):
        for d in order:
            tz = lax.rem(z + d, nz)
            at = rows_at(tz)
            y_copy(s, tz).wait_recv()
            value = y_own[s, at, :] + y_in[s, at, :].astype(f32)
            direct = remote(
                z_out.at[s, at], z_in.at[s, d - 1], z_s.at[s, d - 1], z_r.at[s, d - 1], zdev(tz)
            )
            z_out[s, at, :] = value.astype(bf16)
            if not relay:
                go(direct)
            elif d == 2:
                @pl.when(inner)
                def _():
                    remote(
                        z_rel.at[s], z_rel.at[s], rl_s.at[s], rl_r.at[s], partner
                    ).wait_recv()
                    z_out[s, at, :] = (value + z_rel[s].astype(f32)).astype(bf16)

                go(direct)
            else:
                far = at_last if d == 1 else at_first
                via = z - 1 if d == 1 else z + 1
                go_if(jnp.logical_not(far), direct)
                go_if(far, remote(
                    z_out.at[s, at], z_rel.at[s], rl_s.at[s], rl_r.at[s],
                    zdev(jnp.clip(via, 0, nz - 1)),
                ))

    def residual(s):
        at = rows_at(z)
        y_copy(s, z).wait_recv()
        z_acc[...] = y_own[s, at, :] + y_in[s, at, :].astype(f32)
        for d in order:
            def take(d=d):
                there = z_in.at[s, d - 1]
                remote(there, there, z_s.at[s, d - 1], z_r.at[s, d - 1], partner).wait_recv()
                z_acc[...] += z_in[s, d - 1].astype(f32)

            if relay and d != 2:
                pl.when(jnp.logical_not(at_first if d == 1 else at_last))(take)
            else:
                take()
        value = (emb[rows_at(j), columns(s)].astype(f32) - z_acc[...]).astype(bf16)
        out_res[:, columns(s)] = value
        res[s, place(z, y), :] = value
        here = res.at[s, place(z, y)]
        for d in ([2, 1, 3] if relay else order):
            copy = remote(
                here, here, gz_s.at[s, d - 1], gz_r.at[s, d - 1], zdev(lax.rem(z + d, nz))
            )
            if relay and d != 2:
                go_if(jnp.logical_not(at_last if d == 1 else at_first), copy)
            else:
                go(copy)
        go(remote(here, here, gy_s.at[s, 0], gy_r.at[s, 0], partner))

    def forward(s):
        for d in ([2, 1, 3] if relay else order):
            here = res.at[s, place(lax.rem(z + nz - d, nz), y)]
            remote(here, here, gz_s.at[s, d - 1], gz_r.at[s, d - 1], partner).wait_recv()
            if relay and d == 2:
                go_if(z == 2, remote(here, here, gf_s.at[s], gz_r.at[s, 2], zdev(3)))
                go_if(z == 1, remote(here, here, gf_x.at[s], gz_r.at[s, 0], zdev(0)))
            go(remote(here, here, gy_s.at[s, d], gy_r.at[s, d], partner))

    kb = min(k, 512)

    def update(s):
        for d in range(nz):
            there = res.at[s, place(lax.rem(z + nz - d, nz), 1 - y)]
            remote(there, there, gy_s.at[s, d], gy_r.at[s, d], partner).wait_recv()

        def step(b, _):
            at = pl.ds(pl.multiple_of(b * kb, kb), kb)
            u = jnp.dot(resp_t[at, :], res[s], preferred_element_type=f32)
            if s < n_dp - 1:
                upd_out[s, at, :] = u.astype(bf16)
            else:
                upd_own[at, :] = u
            return 0

        lax.fori_loop(0, k // kb, step, 0)
        if s < n_dp - 1:
            go(remote(
                upd_out.at[s], upd_in.at[s], u_s.at[s], u_r.at[s],
                {"dp": lax.rem(i + 1 + s, n_dp)},
            ))

    def share_rows_dp(buf, s_sem, r_sem):
        for d in range(1, n_dp):
            go(remote(
                buf.at[0], buf.at[d], s_sem.at[d - 1], r_sem.at[d - 1],
                {"dp": lax.rem(i + d, n_dp)},
            ))

    def sum_rows_dp(buf, s_sem, r_sem):
        acc = buf[0]
        for d in range(1, n_dp):
            remote(
                buf.at[0], buf.at[d], s_sem.at[d - 1], r_sem.at[d - 1],
                {"dp": lax.rem(i + d, n_dp)},
            ).wait_recv()
            acc += buf[d]
        return jnp.broadcast_to(acc[0:1], (LANES, k)).T[:, 0:1]

    score_group(0)
    pl.semaphore_wait(barrier, n_cent - 1 + n_dp - 1)
    send_stats(0)
    for g in range(1, groups):
        score_group(g)
        send_stats(g)
    for g in range(groups):
        respond(g)
        mix_group(0, g)
    mix_own(0)
    mix_other(1)
    mix_own(1)
    cnt[0] = lax.dot_general(
        jnp.ones((8, rows), bf16), resp_t[...], (((1,), (1,)), ((), ())),
        preferred_element_type=f32,
    )
    share_rows_dp(cnt, c_s, c_r)

    for t in range(n_dp + 3):
        if t < n_dp:
            z_reduce(t)
        if t + 2 < n_dp:
            mix_other(t + 2)
            mix_own(t + 2)
        if 0 <= t - 1 < n_dp:
            residual(t - 1)
        if 0 <= t - 2 < n_dp:
            forward(t - 2)
        if 0 <= t - 3 < n_dp:
            update(t - 3)

    inv = 1.0 / (sum_rows_dp(cnt, c_s, c_r) + 1.0)
    acc = upd_own[...]
    for s in range(n_dp - 1):
        remote(
            upd_out.at[s], upd_in.at[s], u_s.at[s], u_r.at[s], {"dp": lax.rem(i + 1 + s, n_dp)}
        ).wait_recv()
        acc += upd_in[s].astype(f32)
    own = pl.ds(pl.multiple_of(i * width, LANES), width)
    moved = cent[:, own].astype(f32) + acc * inv
    upd_own[...] = moved
    squares = jnp.sum(moved * moved, axis=1, keepdims=True)
    sq[0] = jnp.broadcast_to(squares, (k, LANES)).T[0:8]
    share_rows_dp(sq, q_s, q_r)
    norm = lax.rsqrt(sum_rows_dp(sq, q_s, q_r) + 1e-06)
    out_cent[...] = upd_own[...] * norm
    for wait in pending:
        wait()


def per_device_fused(n_dp, n_cent, embeddings, sharpness, centroids):
    f32, bf16 = jnp.float32, jnp.bfloat16
    rows, depth = embeddings.shape
    k = centroids.shape[0]
    width = depth // n_dp
    nz = n_cent // 2
    share = rows // n_cent
    half = nz * share
    vmem = pl.BlockSpec(memory_space=pltpu.VMEM)
    dma = lambda *shape: pltpu.SemaphoreType.DMA(shape)
    pairs = lambda *shape: [dma(*shape), dma(*shape)]
    return pl.pallas_call(
        functools.partial(kernel, n_dp, n_cent),
        out_shape=(
            jax.ShapeDtypeStruct((k, width), f32),
            jax.ShapeDtypeStruct((share, depth), bf16),
        ),
        in_specs=[vmem] * 3,
        out_specs=(vmem, vmem),
        scratch_shapes=[
            pltpu.VMEM((k, rows), f32),
            pltpu.VMEM((k, rows), bf16),
            pltpu.VMEM((2, half, k), bf16),
            pltpu.VMEM((nz // 2, n_cent + 1, 2, 4 * share), f32),
            pltpu.VMEM((n_dp, half, width), bf16),
            pltpu.VMEM((n_dp, half, width), bf16),
            pltpu.VMEM((n_dp, half, width), f32),
            pltpu.VMEM((n_dp, half, width), bf16),
            pltpu.VMEM((n_dp, nz - 1, share, width), bf16),
            pltpu.VMEM((n_dp, share, width), bf16),
            pltpu.VMEM((share, width), f32),
            pltpu.VMEM((n_dp, rows, width), bf16),
            pltpu.VMEM((n_dp - 1, k, width), bf16),
            pltpu.VMEM((n_dp - 1, k, width), bf16),
            pltpu.VMEM((k, width), f32),
            pltpu.VMEM((n_dp, 8, k), f32),
            pltpu.VMEM((n_dp, 8, k), f32),
        ]
        + pairs(nz // 2, n_cent - 1)
        + pairs(n_dp, nz)
        + pairs(n_dp, nz - 1)
        + pairs(n_dp)
        + pairs(n_dp, nz - 1)
        + pairs(n_dp)
        + pairs(n_dp, nz)
        + pairs(n_dp - 1)
        + pairs(n_dp - 1)
        + pairs(n_dp - 1),
        compiler_params=pltpu.CompilerParams(
            collective_id=0, has_side_effects=True, vmem_limit_bytes=56 * 2**20
        ),
    )(embeddings, sharpness.reshape(1, rows), centroids)


def solution(mesh):
    n_dp, n_cent = mesh.shape["dp"], mesh.shape["cent"]

    def per_device(embeddings, sharpness, centroids):
        rows, depth = embeddings.shape
        fits = (
            n_dp > 1
            and n_cent % 4 == 0
            and depth % (n_dp * LANES) == 0
            and rows % (n_cent * LANES) == 0
            and centroids.shape[0] % 512 == 0
        )
        if fits:
            return per_device_fused(n_dp, n_cent, embeddings, sharpness, centroids)
        return per_device_plain(embeddings, sharpness, centroids)

    in_specs = (P("dp", None), P("dp"), P("cent", None))
    out_specs = (P("cent", "dp"), P(("dp", "cent"), None))
    return jax.shard_map(
        per_device, mesh=mesh, in_specs=in_specs, out_specs=out_specs, check_vma=False
    )
```

time: 115 us -> 106 us (0.922)
  Pallas kernels: 111 us -> 101 us
    pallas_call x1, Pallas kernels: 111 us -> 101 us  [per_device_fused(): pl.pallas_call(functools.partial(kernel, n_dp, n_cent), out_shape=(jax.Sh...]
where the time goes in v2:
time: 106 us; the launch traced here: 105 us
  Pallas kernels  101 us (95%)
  local copies, waits for them, and re-layouts  3.45 us (3%)
    pallas_call x1, Pallas kernels, per_device_fused(): pl.pallas_call(functools.partial(kernel, n_dp, n_cent), out_shape=(jax.Sh...  101 us
    unnamed x4, local copies, waits for them, and re-layouts  3.45 us

profile of v2, /device:TPU:0, one launch (start us, length us, event | category | flops | bytes accessed | tf_op | source)
XLA Modules:
  0.0 105.5 jit_solution(7583541394347985017)
XLA Ops:
  0.6 101.4 %shard_map.50 = (f32[1024,384]{1,0:T(8,128)}, bf16[128,1536]{1,0:T(8,128)(2,1)}) custom-call(bf16[1024,1536]{1,0:T(8,128)(2,1)} %emb.1, f32[1,1024]{1,0:T(1,128)} %bitcast.1, bf16[1024,1536]{1,0:T(8,128)(2,1)} %cent.1), custom_call_target="tpu_custom_call" | custom-call | tf_op jit(solution)/shard_map/pallas_call | solution.py:350
  102.0 0.0 copy-start
  102.0 2.7 %copy.7 = f32[1024,384]{1,0:T(8,128)} copy(f32[1024,384]{1,0:T(8,128)} %get-tuple-element.4) | data formatting | bytes 3145728
  104.7 0.0 copy-done
  104.7 0.7 copy.8
Async XLA Ops:
  102.0 2.7 %copy-start = (bf16[128,1536]{1,0:T(8,128)(2,1)S(1)}, bf16[128,1536]{1,0:T(8,128)(2,1)}, u32[]{:S(2)}) copy-start(bf16[128,1536]{1,0:T(8,128)(2,1)} %get-tuple-element.5) | copy-start | bytes 1179652

commit v3 on v2

--- a/solution.py
+++ b/solution.py
@@ -52,11 +52,11 @@
 
 
 def kernel(
-    n_dp, n_cent, emb, sharp, cent, out_cent, out_res,
+    n_dp, n_cent, emb_in, sharp, cent_in, out_cent, out_res, emb, cent,
     weights, resp_t, resp, stats, y_out, y_in, y_own, z_out, z_in, z_rel, z_acc, res,
     upd_out, upd_in, upd_own, cnt, sq,
     st_s, st_r, y_s, y_r, z_s, z_r, rl_s, rl_r, gz_s, gz_r, gf_s, gf_x, gy_s, gy_r,
-    u_s, u_r, c_s, c_r, q_s, q_r,
+    hz_s, hz_r, hf_s, u_s, u_r, c_s, c_r, q_s, q_r, e_s,
 ):
     f32, bf16 = jnp.float32, jnp.bfloat16
     rows, depth = emb.shape
@@ -65,8 +65,8 @@
     nz = n_cent // 2
     share = rows // n_cent
     half = nz * share
-    groups = nz // 2
     pair = 2 * share
+    early = n_dp - 2
     relay = nz == 4
     i = lax.axis_index("dp")
     j = lax.axis_index("cent")
@@ -80,7 +80,7 @@
         return pl.ds(pl.multiple_of(index * share, share), share)
 
     def place(zz, yy):
-        return rows_at(yy * nz + zz)
+        return rows_at(zz * 2 + yy)
 
     def zdev(zz):
         return {"cent": zz * 2 + y}
@@ -105,24 +105,28 @@
         pl.when(cond)(copy.start)
         pending.append(lambda: pl.when(cond)(copy.wait_send))
 
+    def pair_rows(g):
+        return pl.ds(g * pair, pair)
+
+    loads = [pltpu.make_async_copy(cent_in, cent, e_s.at[nz])] + [
+        pltpu.make_async_copy(emb_in.at[pair_rows(g)], emb.at[pair_rows(g)], e_s.at[g])
+        for g in range(nz)
+    ]
+    for load in loads:
+        load.start()
+    loads[0].wait()
+
     def score_group(g):
-        def half_block(h, _):
-            e = jnp.concatenate([emb[rows_at(4 * g + h), :], emb[rows_at(4 * g + 2 + h), :]], 0)
-            sh = jnp.concatenate(
-                [sharp[:, rows_at(4 * g + h)], sharp[:, rows_at(4 * g + 2 + h)]], 1
-            )
-            s = lax.dot_general(
-                cent[...], e, (((1,), (1,)), ((), ())), preferred_element_type=f32
-            ) * sh
-            top = jnp.max(s, axis=0, keepdims=True)
-            w = jnp.exp(s - top)
-            weights[:, pl.ds(pl.multiple_of(h * half + g * pair, share), pair)] = w
-            at = pl.ds(pl.multiple_of(h * pair, share), pair)
-            stats[g, j, 0:1, at] = top
-            stats[g, j, 1:2, at] = jnp.sum(w, axis=0, keepdims=True)
-            return 0
-
-        lax.fori_loop(0, 2, half_block, 0)
+        loads[1 + g].wait()
+        at = pair_rows(g)
+        s = lax.dot_general(
+            cent[...], emb[at, :], (((1,), (1,)), ((), ())), preferred_element_type=f32
+        ) * sharp[:, at]
+        top = jnp.max(s, axis=0, keepdims=True)
+        w = jnp.exp(s - top)
+        weights[:, at] = w
+        stats[g, j, 0:1, :] = top
+        stats[g, j, 1:2, :] = jnp.sum(w, axis=0, keepdims=True)
 
     def send_stats(g):
         here = stats.at[g, j]
@@ -141,17 +145,11 @@
         total = functools.reduce(
             jnp.add, [stats[g, c, 1:2, :] * jnp.exp(tops[c] - top) for c in range(n_cent)]
         )
-        stats[g, n_cent, 0:1, :] = jnp.exp(stats[g, j, 0:1, :] - top) / total
-
-        def block(b, _):
-            h, q = b // 2, b % 2
-            at = place(2 * g + q, h)
-            r = weights[:, at] * stats[g, n_cent, 0:1, rows_at(b)]
-            resp_t[:, at] = r.astype(bf16)
-            resp[h, rows_at(2 * g + q), :] = r.T.astype(bf16)
-            return 0
-
-        lax.fori_loop(0, 4, block, 0)
+        scale = jnp.exp(stats[g, j, 0:1, :] - top) / total
+        r = weights[:, pair_rows(g)] * scale
+        resp_t[:, pair_rows(g)] = r.astype(bf16)
+        for h in range(2):
+            resp[h, rows_at(g), :] = r[:, h * share:(h + 1) * share].T.astype(bf16)
 
     def columns(s):
         owner = lax.rem(i + 1 + s, n_dp)
@@ -162,12 +160,11 @@
         return remote(y_out.at[s, at], y_in.at[s, at], y_s.at[s, zz], y_r.at[s, zz], partner)
 
     def mix_group(s, g):
-        at = pl.ds(g * pair, pair)
+        at = rows_at(g)
         y_out[s, at, :] = jnp.dot(
             resp[1 - y, at, :], cent[:, columns(s)], preferred_element_type=f32
         ).astype(bf16)
-        for q in range(2):
-            go(y_copy(s, 2 * g + q))
+        go(y_copy(s, g))
 
     def mix_other(s):
         y_out[s] = jnp.dot(
@@ -227,29 +224,48 @@
         out_res[:, columns(s)] = value
         res[s, place(z, y), :] = value
         here = res.at[s, place(z, y)]
-        for d in ([2, 1, 3] if relay else order):
-            copy = remote(
-                here, here, gz_s.at[s, d - 1], gz_r.at[s, d - 1], zdev(lax.rem(z + d, nz))
-            )
+        if s == early:
+            go(remote(here, here, gy_s.at[s, 0], gy_r.at[s, 0], partner))
+        spread(here, lambda d: (gz_s.at[s, d - 1], gz_r.at[s, d - 1]))
+        if s != early:
+            go(remote(here, here, gy_s.at[s, 0], gy_r.at[s, 0], partner))
+
+    z_order = [2, 1, 3] if relay else order
+
+    def spread(here, sems):
+        for d in z_order:
+            copy = remote(here, here, *sems(d), zdev(lax.rem(z + d, nz)))
             if relay and d != 2:
                 go_if(jnp.logical_not(at_last if d == 1 else at_first), copy)
             else:
                 go(copy)
-        go(remote(here, here, gy_s.at[s, 0], gy_r.at[s, 0], partner))
+
+    def arrive(s, d, yy, sems, onward):
+        here = res.at[s, place(lax.rem(z + nz - d, nz), yy)]
+        remote(here, here, *sems(d), partner).wait_recv()
+        if relay and d == 2:
+            go_if(z == 2, remote(here, here, onward(0), sems(3)[1], zdev(3)))
+            go_if(z == 1, remote(here, here, onward(1), sems(1)[1], zdev(0)))
+        return here
 
     def forward(s):
-        for d in ([2, 1, 3] if relay else order):
-            here = res.at[s, place(lax.rem(z + nz - d, nz), y)]
-            remote(here, here, gz_s.at[s, d - 1], gz_r.at[s, d - 1], partner).wait_recv()
-            if relay and d == 2:
-                go_if(z == 2, remote(here, here, gf_s.at[s], gz_r.at[s, 2], zdev(3)))
-                go_if(z == 1, remote(here, here, gf_x.at[s], gz_r.at[s, 0], zdev(0)))
-            go(remote(here, here, gy_s.at[s, d], gy_r.at[s, d], partner))
+        own = lambda d: (gz_s.at[s, d - 1], gz_r.at[s, d - 1])
+        other = lambda d: (hz_s.at[d - 1], hz_r.at[d - 1])
+        if s == early:
+            here = res.at[s, place(z, 1 - y)]
+            remote(here, here, gy_s.at[s, 0], gy_r.at[s, 0], partner).wait_recv()
+            spread(here, other)
+        for d in z_order:
+            here = arrive(s, d, y, own, lambda way: (gf_s if way == 0 else gf_x).at[s])
+            if s == early:
+                arrive(s, d, 1 - y, other, lambda way: hf_s.at[way])
+            else:
+                go(remote(here, here, gy_s.at[s, d], gy_r.at[s, d], partner))
 
     kb = min(k, 512)
 
     def update(s):
-        for d in range(nz):
+        for d in range(nz if s != early else 0):
             there = res.at[s, place(lax.rem(z + nz - d, nz), 1 - y)]
             remote(there, there, gy_s.at[s, d], gy_r.at[s, d], partner).wait_recv()
 
@@ -289,12 +305,16 @@
     score_group(0)
     pl.semaphore_wait(barrier, n_cent - 1 + n_dp - 1)
     send_stats(0)
-    for g in range(1, groups):
+    lead = min(3, nz)
+    for g in range(1, lead):
         score_group(g)
         send_stats(g)
-    for g in range(groups):
+    for g in range(nz):
         respond(g)
         mix_group(0, g)
+        if g + lead < nz:
+            score_group(g + lead)
+            send_stats(g + lead)
     mix_own(0)
     mix_other(1)
     mix_own(1)
@@ -336,6 +356,18 @@
         wait()
 
 
+def hand_over(pieces, a, b, out_a, out_b, sem):
+    size = a.shape[0] // pieces
+    copies = [pltpu.make_async_copy(b, out_b, sem.at[pieces])]
+    for p in range(pieces):
+        at = pl.ds(p * size, size)
+        copies.append(pltpu.make_async_copy(a.at[at], out_a.at[at], sem.at[p]))
+    for copy in copies:
+        copy.start()
+    for copy in copies:
+        copy.wait()
+
+
 def per_device_fused(n_dp, n_cent, embeddings, sharpness, centroids):
     f32, bf16 = jnp.float32, jnp.bfloat16
     rows, depth = embeddings.shape
@@ -345,21 +377,24 @@
     share = rows // n_cent
     half = nz * share
     vmem = pl.BlockSpec(memory_space=pltpu.VMEM)
+    hbm = pl.BlockSpec(memory_space=pl.ANY)
     dma = lambda *shape: pltpu.SemaphoreType.DMA(shape)
     pairs = lambda *shape: [dma(*shape), dma(*shape)]
-    return pl.pallas_call(
+    moved, own = pl.pallas_call(
         functools.partial(kernel, n_dp, n_cent),
         out_shape=(
             jax.ShapeDtypeStruct((k, width), f32),
             jax.ShapeDtypeStruct((share, depth), bf16),
         ),
-        in_specs=[vmem] * 3,
+        in_specs=[hbm, vmem, hbm],
         out_specs=(vmem, vmem),
         scratch_shapes=[
+            pltpu.VMEM((rows, depth), bf16),
+            pltpu.VMEM((k, depth), bf16),
             pltpu.VMEM((k, rows), f32),
             pltpu.VMEM((k, rows), bf16),
             pltpu.VMEM((2, half, k), bf16),
-            pltpu.VMEM((nz // 2, n_cent + 1, 2, 4 * share), f32),
+            pltpu.VMEM((nz, n_cent, 2, 2 * share), f32),
             pltpu.VMEM((n_dp, half, width), bf16),
             pltpu.VMEM((n_dp, half, width), bf16),
             pltpu.VMEM((n_dp, half, width), f32),
@@ -374,20 +409,34 @@
             pltpu.VMEM((n_dp, 8, k), f32),
             pltpu.VMEM((n_dp, 8, k), f32),
         ]
-        + pairs(nz // 2, n_cent - 1)
+        + pairs(nz, n_cent - 1)
         + pairs(n_dp, nz)
         + pairs(n_dp, nz - 1)
         + pairs(n_dp)
         + pairs(n_dp, nz - 1)
         + pairs(n_dp)
         + pairs(n_dp, nz)
+        + pairs(nz - 1)
+        + [dma(2)]
         + pairs(n_dp - 1)
         + pairs(n_dp - 1)
-        + pairs(n_dp - 1),
+        + pairs(n_dp - 1)
+        + [dma(nz + 1)],
         compiler_params=pltpu.CompilerParams(
             collective_id=0, has_side_effects=True, vmem_limit_bytes=56 * 2**20
         ),
     )(embeddings, sharpness.reshape(1, rows), centroids)
+    pieces = 4
+    return pl.pallas_call(
+        functools.partial(hand_over, pieces),
+        out_shape=(
+            jax.ShapeDtypeStruct((k, width), f32),
+            jax.ShapeDtypeStruct((share, depth), bf16),
+        ),
+        in_specs=[hbm, hbm],
+        out_specs=(hbm, hbm),
+        scratch_shapes=[dma(pieces + 1)],
+    )(moved, own)
 
 
 def solution(mesh):

time: 106 us -> 176 us (1.66)
  Pallas kernels: 101 us -> 175 us
  local copies, waits for them, and re-layouts: 3.45 us -> 0 us
    pallas_call x0 -> x1, Pallas kernels: none -> 60.7 us  [per_device_fused(): pl.pallas_call(functools.partial(hand_over, pieces), out_shape=(jax.Shape...]
    pallas_call x1, Pallas kernels: 101 us -> 115 us  [per_device_fused(): pl.pallas_call(functools.partial(kernel, n_dp, n_cent), out_shape=(jax.Sh...]
    unnamed x4 -> x0, local copies, waits for them, and re-layouts: 3.45 us -> none
where the time goes in v3:
time: 176 us
  Pallas kernels  175 us (99%)
    pallas_call x1, Pallas kernels, per_device_fused(): pl.pallas_call(functools.partial(kernel, n_dp, n_cent), out_shape=(jax.Sh...  115 us
    pallas_call x1, Pallas kernels, per_device_fused(): pl.pallas_call(functools.partial(hand_over, pieces), out_shape=(jax.Shape...  60.7 us

profile of v3, /device:TPU:0, one launch (start us, length us, event | category | flops | bytes accessed | tf_op | source)
XLA Modules:
  0.0 176.1 jit_solution(2306622024646371832)
XLA Ops:
  0.6 114.6 %shard_map.50 = (f32[1024,384]{1,0:T(8,128)}, bf16[128,1536]{1,0:T(8,128)(2,1)}) custom-call(bf16[1024,1536]{1,0:T(8,128)(2,1)} %emb_in.1, f32[1,1024]{1,0:T(1,128)} %bitcast.1, bf16[1024,1536]{1,0:T(8,128)(2,1)} %cent_in.1), custom_call_target="tpu_custom_call" | custom-call | tf_op jit(solution)/shard_map/pallas_call | solution.py:383
  115.2 60.7 %shard_map.51 = (f32[1024,384]{1,0:T(8,128)}, bf16[128,1536]{1,0:T(8,128)(2,1)}) custom-call(f32[1024,384]{1,0:T(8,128)} %get-tuple-element.4.a, bf16[128,1536]{1,0:T(8,128)(2,1)} %get-tuple-element.5.b), custom_call_target="tpu_custom_call" | custom-call | tf_op jit(solution)/shard_map/pallas_call | solution.py:430

commit v4 on v3

--- a/solution.py
+++ b/solution.py
@@ -56,7 +56,7 @@
     weights, resp_t, resp, stats, y_out, y_in, y_own, z_out, z_in, z_rel, z_acc, res,
     upd_out, upd_in, upd_own, cnt, sq,
     st_s, st_r, y_s, y_r, z_s, z_r, rl_s, rl_r, gz_s, gz_r, gf_s, gf_x, gy_s, gy_r,
-    hz_s, hz_r, hf_s, u_s, u_r, c_s, c_r, q_s, q_r, e_s,
+    u_s, u_r, c_s, c_r, q_s, q_r, e_s,
 ):
     f32, bf16 = jnp.float32, jnp.bfloat16
     rows, depth = emb.shape
@@ -66,7 +66,6 @@
     share = rows // n_cent
     half = nz * share
     pair = 2 * share
-    early = n_dp - 2
     relay = nz == 4
     i = lax.axis_index("dp")
     j = lax.axis_index("cent")
@@ -224,11 +223,8 @@
         out_res[:, columns(s)] = value
         res[s, place(z, y), :] = value
         here = res.at[s, place(z, y)]
-        if s == early:
-            go(remote(here, here, gy_s.at[s, 0], gy_r.at[s, 0], partner))
         spread(here, lambda d: (gz_s.at[s, d - 1], gz_r.at[s, d - 1]))
-        if s != early:
-            go(remote(here, here, gy_s.at[s, 0], gy_r.at[s, 0], partner))
+        go(remote(here, here, gy_s.at[s, 0], gy_r.at[s, 0], partner))
 
     z_order = [2, 1, 3] if relay else order
 
@@ -240,32 +236,19 @@
             else:
                 go(copy)
 
-    def arrive(s, d, yy, sems, onward):
-        here = res.at[s, place(lax.rem(z + nz - d, nz), yy)]
-        remote(here, here, *sems(d), partner).wait_recv()
-        if relay and d == 2:
-            go_if(z == 2, remote(here, here, onward(0), sems(3)[1], zdev(3)))
-            go_if(z == 1, remote(here, here, onward(1), sems(1)[1], zdev(0)))
-        return here
-
     def forward(s):
-        own = lambda d: (gz_s.at[s, d - 1], gz_r.at[s, d - 1])
-        other = lambda d: (hz_s.at[d - 1], hz_r.at[d - 1])
-        if s == early:
-            here = res.at[s, place(z, 1 - y)]
-            remote(here, here, gy_s.at[s, 0], gy_r.at[s, 0], partner).wait_recv()
-            spread(here, other)
         for d in z_order:
-            here = arrive(s, d, y, own, lambda way: (gf_s if way == 0 else gf_x).at[s])
-            if s == early:
-                arrive(s, d, 1 - y, other, lambda way: hf_s.at[way])
-            else:
-                go(remote(here, here, gy_s.at[s, d], gy_r.at[s, d], partner))
+            here = res.at[s, place(lax.rem(z + nz - d, nz), y)]
+            remote(here, here, gz_s.at[s, d - 1], gz_r.at[s, d - 1], partner).wait_recv()
+            if relay and d == 2:
+                go_if(z == 2, remote(here, here, gf_s.at[s], gz_r.at[s, 2], zdev(3)))
+                go_if(z == 1, remote(here, here, gf_x.at[s], gz_r.at[s, 0], zdev(0)))
+            go(remote(here, here, gy_s.at[s, d], gy_r.at[s, d], partner))
 
     kb = min(k, 512)
 
     def update(s):
-        for d in range(nz if s != early else 0):
+        for d in range(nz):
             there = res.at[s, place(lax.rem(z + nz - d, nz), 1 - y)]
             remote(there, there, gy_s.at[s, d], gy_r.at[s, d], partner).wait_recv()
 
@@ -356,16 +339,9 @@
         wait()
 
 
-def hand_over(pieces, a, b, out_a, out_b, sem):
-    size = a.shape[0] // pieces
-    copies = [pltpu.make_async_copy(b, out_b, sem.at[pieces])]
-    for p in range(pieces):
-        at = pl.ds(p * size, size)
-        copies.append(pltpu.make_async_copy(a.at[at], out_a.at[at], sem.at[p]))
-    for copy in copies:
-        copy.start()
-    for copy in copies:
-        copy.wait()
+def hand_over(a, b, out_a, out_b):
+    out_a[...] = a[...]
+    out_b[...] = b[...]
 
 
 def per_device_fused(n_dp, n_cent, embeddings, sharpness, centroids):
@@ -416,8 +392,6 @@
         + pairs(n_dp, nz - 1)
         + pairs(n_dp)
         + pairs(n_dp, nz)
-        + pairs(nz - 1)
-        + [dma(2)]
         + pairs(n_dp - 1)
         + pairs(n_dp - 1)
         + pairs(n_dp - 1)
@@ -426,16 +400,20 @@
             collective_id=0, has_side_effects=True, vmem_limit_bytes=56 * 2**20
         ),
     )(embeddings, sharpness.reshape(1, rows), centroids)
-    pieces = 4
+    steps = 4
+    blocks = [
+        pl.BlockSpec((k // steps, width), lambda t: (t, 0)),
+        pl.BlockSpec((share // steps, depth), lambda t: (t, 0)),
+    ]
     return pl.pallas_call(
-        functools.partial(hand_over, pieces),
+        hand_over,
+        grid=(steps,),
         out_shape=(
             jax.ShapeDtypeStruct((k, width), f32),
             jax.ShapeDtypeStruct((share, depth), bf16),
         ),
-        in_specs=[hbm, hbm],
-        out_specs=(hbm, hbm),
-        scratch_shapes=[dma(pieces + 1)],
+        in_specs=blocks,
+        out_specs=tuple(blocks),
     )(moved, own)
 
 

time: 176 us -> 111 us (0.63)
  Pallas kernels: 175 us -> 110 us
    pallas_call x1, Pallas kernels: 60.7 us -> 3.67 us  [per_device_fused(): pl.pallas_call(hand_over, grid=(steps,), out_shape=(jax.ShapeDtypeStruct(...]
    pallas_call x1, Pallas kernels: 115 us -> 106 us  [per_device_fused(): pl.pallas_call(functools.partial(kernel, n_dp, n_cent), out_shape=(jax.Sh...]
where the time goes in v4:
time: 111 us
  Pallas kernels  110 us (99%)
    pallas_call x1, Pallas kernels, per_device_fused(): pl.pallas_call(functools.partial(kernel, n_dp, n_cent), out_shape=(jax.Sh...  106 us
    pallas_call x1, Pallas kernels, per_device_fused(): pl.pallas_call(hand_over, grid=(steps,), out_shape=(jax.ShapeDtypeStruct(...  3.67 us

profile of v4, /device:TPU:0, one launch (start us, length us, event | category | flops | bytes accessed | tf_op | source)
XLA Modules:
  0.0 110.6 jit_solution(11140711197485743439)
XLA Ops:
  0.6 106.2 %shard_map.50 = (f32[1024,384]{1,0:T(8,128)}, bf16[128,1536]{1,0:T(8,128)(2,1)}) custom-call(bf16[1024,1536]{1,0:T(8,128)(2,1)} %emb_in.1, f32[1,1024]{1,0:T(1,128)} %bitcast.1, bf16[1024,1536]{1,0:T(8,128)(2,1)} %cent_in.1), custom_call_target="tpu_custom_call" | custom-call | tf_op jit(solution)/shard_map/pallas_call | solution.py:359
  106.9 3.7 %shard_map.51 = (f32[1024,384]{1,0:T(8,128)}, bf16[128,1536]{1,0:T(8,128)(2,1)}) custom-call(f32[1024,384]{1,0:T(8,128)} %get-tuple-element.4.a, bf16[128,1536]{1,0:T(8,128)(2,1)} %get-tuple-element.5.b), custom_call_target="tpu_custom_call" | custom-call | tf_op jit(solution)/shard_map/pallas_call | solution.py:408

commit v5 on v2

--- a/solution.py
+++ b/solution.py
@@ -53,7 +53,7 @@
 
 def kernel(
     n_dp, n_cent, emb, sharp, cent, out_cent, out_res,
-    weights, resp_t, resp, stats, y_out, y_in, y_own, z_out, z_in, z_rel, z_acc, res,
+    weights, resp_t, resp, scales, stats, y_out, y_in, y_own, z_out, z_in, z_rel, z_acc, res,
     upd_out, upd_in, upd_own, cnt, sq,
     st_s, st_r, y_s, y_r, z_s, z_r, rl_s, rl_r, gz_s, gz_r, gf_s, gf_x, gy_s, gy_r,
     u_s, u_r, c_s, c_r, q_s, q_r,
@@ -118,6 +118,7 @@
             w = jnp.exp(s - top)
             weights[:, pl.ds(pl.multiple_of(h * half + g * pair, share), pair)] = w
             at = pl.ds(pl.multiple_of(h * pair, share), pair)
+            resp[h, pl.ds(g * pair, pair), :] = w.T.astype(bf16)
             stats[g, j, 0:1, at] = top
             stats[g, j, 1:2, at] = jnp.sum(w, axis=0, keepdims=True)
             return 0
@@ -142,13 +143,18 @@
             jnp.add, [stats[g, c, 1:2, :] * jnp.exp(tops[c] - top) for c in range(n_cent)]
         )
         stats[g, n_cent, 0:1, :] = jnp.exp(stats[g, j, 0:1, :] - top) / total
+        stats[g, n_cent, 1:2, :] = jnp.exp(stats[g, z * 2 + 1 - y, 0:1, :] - top) / total
+        mine = pl.ds(pl.multiple_of(y * pair, share), pair)
+        for who in range(2):
+            scales[who, pl.ds(g * pair, pair), :] = jnp.broadcast_to(
+                stats[g, n_cent, who:who + 1, mine], (LANES, pair)
+            ).T
 
         def block(b, _):
             h, q = b // 2, b % 2
             at = place(2 * g + q, h)
             r = weights[:, at] * stats[g, n_cent, 0:1, rows_at(b)]
             resp_t[:, at] = r.astype(bf16)
-            resp[h, rows_at(2 * g + q), :] = r.T.astype(bf16)
             return 0
 
         lax.fori_loop(0, 4, block, 0)
@@ -179,12 +185,18 @@
     def mix_own(s):
         y_own[s] = jnp.dot(resp[y], cent[:, columns(s)], preferred_element_type=f32)
 
+    def y_sum(s, at):
+        return (
+            y_own[s, at, :] * scales[0, at, 0:1]
+            + y_in[s, at, :].astype(f32) * scales[1, at, 0:1]
+        )
+
     def z_reduce(s):
         for d in order:
             tz = lax.rem(z + d, nz)
             at = rows_at(tz)
             y_copy(s, tz).wait_recv()
-            value = y_own[s, at, :] + y_in[s, at, :].astype(f32)
+            value = y_sum(s, at)
             direct = remote(
                 z_out.at[s, at], z_in.at[s, d - 1], z_s.at[s, d - 1], z_r.at[s, d - 1], zdev(tz)
             )
@@ -212,7 +224,7 @@
     def residual(s):
         at = rows_at(z)
         y_copy(s, z).wait_recv()
-        z_acc[...] = y_own[s, at, :] + y_in[s, at, :].astype(f32)
+        z_acc[...] = y_sum(s, at)
         for d in order:
             def take(d=d):
                 there = z_in.at[s, d - 1]
@@ -289,15 +301,16 @@
     score_group(0)
     pl.semaphore_wait(barrier, n_cent - 1 + n_dp - 1)
     send_stats(0)
+    mix_group(0, 0)
     for g in range(1, groups):
         score_group(g)
         send_stats(g)
-    for g in range(groups):
-        respond(g)
         mix_group(0, g)
     mix_own(0)
     mix_other(1)
     mix_own(1)
+    for g in range(groups):
+        respond(g)
     cnt[0] = lax.dot_general(
         jnp.ones((8, rows), bf16), resp_t[...], (((1,), (1,)), ((), ())),
         preferred_element_type=f32,
@@ -359,6 +372,7 @@
             pltpu.VMEM((k, rows), f32),
             pltpu.VMEM((k, rows), bf16),
             pltpu.VMEM((2, half, k), bf16),
+            pltpu.VMEM((2, half, LANES), f32),
             pltpu.VMEM((nz // 2, n_cent + 1, 2, 4 * share), f32),
             pltpu.VMEM((n_dp, half, width), bf16),
             pltpu.VMEM((n_dp, half, width), bf16),

time: 106 us -> 108 us (1.019)
  Pallas kernels: 101 us -> 104 us
    pallas_call x1, Pallas kernels: 101 us -> 104 us  [per_device_fused(): pl.pallas_call(functools.partial(kernel, n_dp, n_cent), out_shape=(jax.Sh...]
where the time goes in v5:
time: 108 us
  Pallas kernels  104 us (96%)
  local copies, waits for them, and re-layouts  3.45 us (3%)
    pallas_call x1, Pallas kernels, per_device_fused(): pl.pallas_call(functools.partial(kernel, n_dp, n_cent), out_shape=(jax.Sh...  104 us
    unnamed x4, local copies, waits for them, and re-layouts  3.45 us

profile of v5, /device:TPU:0, one launch (start us, length us, event | category | flops | bytes accessed | tf_op | source)
XLA Modules:
  0.0 108.3 jit_solution(8298206102782919427)
XLA Ops:
  0.6 104.2 %shard_map.50 = (f32[1024,384]{1,0:T(8,128)}, bf16[128,1536]{1,0:T(8,128)(2,1)}) custom-call(bf16[1024,1536]{1,0:T(8,128)(2,1)} %emb.1, f32[1,1024]{1,0:T(1,128)} %bitcast.1, bf16[1024,1536]{1,0:T(8,128)(2,1)} %cent.1), custom_call_target="tpu_custom_call" | custom-call | tf_op jit(solution)/shard_map/pallas_call | solution.py:363
  104.9 0.0 copy-start
  104.9 2.7 %copy.7 = f32[1024,384]{1,0:T(8,128)} copy(f32[1024,384]{1,0:T(8,128)} %get-tuple-element.4) | data formatting | bytes 3145728
  107.6 0.0 copy-done
  107.6 0.7 copy.8
Async XLA Ops:
  104.9 2.7 %copy-start = (bf16[128,1536]{1,0:T(8,128)(2,1)S(1)}, bf16[128,1536]{1,0:T(8,128)(2,1)}, u32[]{:S(2)}) copy-start(bf16[128,1536]{1,0:T(8,128)(2,1)} %get-tuple-element.5) | copy-start | bytes 1179652

commit v6 on v2

--- a/solution.py
+++ b/solution.py
@@ -72,6 +72,10 @@
     j = lax.axis_index("cent")
     z, y = j // 2, j % 2
     partner = {"cent": z * 2 + (1 - y)}
+    ix, ic = i // 2, i % 2
+    sibling = ix * 2 + (1 - ic)
+    owners = [(1 - ix) * 2 + (1 - ic), (1 - ix) * 2 + ic, sibling, i]
+    targets = [sibling, owners[1], sibling]
     inner = jnp.logical_and(z > 0, z < nz - 1)
     at_first, at_last = z == 0, z == nz - 1
     order = [nz - 1] + list(range(1, nz - 1)) if nz > 2 else [1]
@@ -154,8 +158,7 @@
         lax.fori_loop(0, 4, block, 0)
 
     def columns(s):
-        owner = lax.rem(i + 1 + s, n_dp)
-        return pl.ds(pl.multiple_of(owner * width, LANES), width)
+        return pl.ds(pl.multiple_of(owners[s] * width, LANES), width)
 
     def y_copy(s, zz):
         at = rows_at(zz)
@@ -253,9 +256,16 @@
             there = res.at[s, place(lax.rem(z + nz - d, nz), 1 - y)]
             remote(there, there, gy_s.at[s, d], gy_r.at[s, d], partner).wait_recv()
 
+        if s == 1:
+            remote(
+                upd_out.at[0], upd_in.at[0], u_s.at[0], u_r.at[0], {"dp": targets[0]}
+            ).wait_recv()
+
         def step(b, _):
             at = pl.ds(pl.multiple_of(b * kb, kb), kb)
             u = jnp.dot(resp_t[at, :], res[s], preferred_element_type=f32)
+            if s == 1:
+                u = u + upd_in[0, at, :].astype(f32)
             if s < n_dp - 1:
                 upd_out[s, at, :] = u.astype(bf16)
             else:
@@ -265,8 +275,7 @@
         lax.fori_loop(0, k // kb, step, 0)
         if s < n_dp - 1:
             go(remote(
-                upd_out.at[s], upd_in.at[s], u_s.at[s], u_r.at[s],
-                {"dp": lax.rem(i + 1 + s, n_dp)},
+                upd_out.at[s], upd_in.at[s], u_s.at[s], u_r.at[s], {"dp": targets[s]},
             ))
 
     def share_rows_dp(buf, s_sem, r_sem):
@@ -319,9 +328,9 @@
 
     inv = 1.0 / (sum_rows_dp(cnt, c_s, c_r) + 1.0)
     acc = upd_own[...]
-    for s in range(n_dp - 1):
+    for s in range(1, n_dp - 1):
         remote(
-            upd_out.at[s], upd_in.at[s], u_s.at[s], u_r.at[s], {"dp": lax.rem(i + 1 + s, n_dp)}
+            upd_out.at[s], upd_in.at[s], u_s.at[s], u_r.at[s], {"dp": targets[s]}
         ).wait_recv()
         acc += upd_in[s].astype(f32)
     own = pl.ds(pl.multiple_of(i * width, LANES), width)
@@ -396,7 +405,7 @@
     def per_device(embeddings, sharpness, centroids):
         rows, depth = embeddings.shape
         fits = (
-            n_dp > 1
+            n_dp == 4
             and n_cent % 4 == 0
             and depth % (n_dp * LANES) == 0
             and rows % (n_cent * LANES) == 0

time: 106 us -> 101 us (0.953)
  Pallas kernels: 101 us -> 97 us
    pallas_call x1, Pallas kernels: 101 us -> 97 us  [per_device_fused(): pl.pallas_call(functools.partial(kernel, n_dp, n_cent), out_shape=(jax.Sh...]
where the time goes in v6:
time: 101 us
  Pallas kernels  97 us (96%)
  local copies, waits for them, and re-layouts  3.45 us (3%)
    pallas_call x1, Pallas kernels, per_device_fused(): pl.pallas_call(functools.partial(kernel, n_dp, n_cent), out_shape=(jax.Sh...  97 us
    unnamed x4, local copies, waits for them, and re-layouts  3.45 us

profile of v6, /device:TPU:0, one launch (start us, length us, event | category | flops | bytes accessed | tf_op | source)
XLA Modules:
  0.0 101.1 jit_solution(13794159745677176533)
XLA Ops:
  0.6 97.0 %shard_map.50 = (f32[1024,384]{1,0:T(8,128)}, bf16[128,1536]{1,0:T(8,128)(2,1)}) custom-call(bf16[1024,1536]{1,0:T(8,128)(2,1)} %emb.1, f32[1,1024]{1,0:T(1,128)} %bitcast.1, bf16[1024,1536]{1,0:T(8,128)(2,1)} %cent.1), custom_call_target="tpu_custom_call" | custom-call | tf_op jit(solution)/shard_map/pallas_call | solution.py:359
  97.6 0.0 copy-start
  97.7 2.7 %copy.7 = f32[1024,384]{1,0:T(8,128)} copy(f32[1024,384]{1,0:T(8,128)} %get-tuple-element.4) | data formatting | bytes 3145728
  100.4 0.0 copy-done
  100.4 0.7 copy.8
Async XLA Ops:
  97.6 2.7 %copy-start = (bf16[128,1536]{1,0:T(8,128)(2,1)S(1)}, bf16[128,1536]{1,0:T(8,128)(2,1)}, u32[]{:S(2)}) copy-start(bf16[128,1536]{1,0:T(8,128)(2,1)} %get-tuple-element.5) | copy-start | bytes 1179652
